TPU v7x, 32 devices: a whole 2x2x4 slice. The times are simulated.
32 devices in a mesh: dp: 4 (over x, core), mx: 4 (over z), my: 2 (over y).
Axes of the slice: x: 2, y: 2, z: 4, core: 2. Of those that a mesh axis runs over, the one named last changes fastest.
Arguments:
- tokens: bfloat16 [1024, 6144], P('dp', ('mx', 'my')), may hold values from -6 to 6
- cotangent: bfloat16 [1024, 6144], P('dp', ('mx', 'my')), may hold values from -1.1953125 to 1.1953125
- w_in: bfloat16 [6144, 12288], P('mx', 'my'), may hold values from -0.078125 to 0.078125
- w_out: bfloat16 [12288, 6144], P('my', 'mx'), may hold values from -0.0546875 to 0.0546875
Outputs:
- output: bfloat16 [1024, 6144], P('dp', ('mx', 'my'))
- input_grad: bfloat16 [1024, 6144], P('dp', ('mx', 'my'))
- w_in_grad: bfloat16 [6144, 12288], P('mx', ('my', 'dp'))
- w_out_grad: bfloat16 [12288, 6144], P(('my', 'dp'), 'mx')
All inputs are finite; a program needn't handle non-finite values.
Results may differ from a plain program's by a relative error of at most 0.019.
Values may be sent and summed in bfloat16 or wider, within the bound.
A program may use at most 192 MiB of HBM per device.

v0:
```python
import jax
import jax.numpy as jnp
from jax import lax
from jax.sharding import PartitionSpec as P


def gelu_parts(hidden):
    cdf = 0.5 * (1.0 + lax.erf(hidden * 0.7071067811865476))
    density = jnp.exp(-0.5 * hidden * hidden) * 0.3989422804014327
    return (hidden * cdf, cdf + hidden * density)


def per_device(tokens, cotangent, w_in, w_out):
    columns = lax.all_gather(tokens, "my", axis=1, tiled=True)
    hidden_part = jnp.dot(columns, w_in, preferred_element_type=jnp.float32)
    hidden = lax.psum(hidden_part.astype(jnp.bfloat16), "mx").astype(jnp.float32)
    act_full, slope = gelu_parts(hidden)
    active = act_full.astype(jnp.bfloat16)
    out_part = jnp.dot(active, w_out, preferred_element_type=jnp.float32)
    output = lax.psum_scatter(out_part.astype(jnp.bfloat16), "my", scatter_dimension=1, tiled=True)
    grad_cols = lax.all_gather(cotangent, "my", axis=1, tiled=True)
    act_part = lax.dot_general(
        grad_cols, w_out, (((1,), (1,)), ((), ())), preferred_element_type=jnp.float32
    )
    act_grad = lax.psum(act_part.astype(jnp.bfloat16), "mx").astype(jnp.float32)
    hidden_grad = (act_grad * slope).astype(jnp.bfloat16)
    input_part = lax.dot_general(
        hidden_grad, w_in, (((1,), (1,)), ((), ())), preferred_element_type=jnp.float32
    )
    input_grad = lax.psum_scatter(
        input_part.astype(jnp.bfloat16), "my", scatter_dimension=1, tiled=True
    )
    in_part = lax.dot_general(
        columns, hidden_grad, (((0,), (0,)), ((), ())), preferred_element_type=jnp.float32
    )
    out_term = lax.dot_general(
        active, grad_cols, (((0,), (0,)), ((), ())), preferred_element_type=jnp.float32
    )
    w_in_grad = lax.psum_scatter(
        in_part.astype(jnp.bfloat16), "dp", scatter_dimension=1, tiled=True
    )
    w_out_grad = lax.psum_scatter(
        out_term.astype(jnp.bfloat16), "dp", scatter_dimension=0, tiled=True
    )
    return (output, input_grad, w_in_grad, w_out_grad)


def solution(mesh):
    in_specs = (P("dp", ("mx", "my")), P("dp", ("mx", "my")), P("mx", "my"), P("my", "mx"))
    out_specs = (
        P("dp", ("mx", "my")),
        P("dp", ("mx", "my")),
        P("mx", ("my", "dp")),
        P(("my", "dp"), "mx"),
    )
    return jax.shard_map(
        per_device, mesh=mesh, in_specs=in_specs, out_specs=out_specs, check_vma=False
    )
```

profile of v0, /device:TPU:0, one launch (start us, length us, event | category | flops | bytes accessed | tf_op | source)
XLA Modules:
  0.0 620.6 jit_solution(13184943301326188222)
XLA Ops:
  7.2 0.0 all-reduce.3.cloned.1.call-start
  7.2 13.0 %all_gather.6 = bf16[256,1536]{1,0:T(8,128)(2,1)S(1)} all-gather(bf16[256,768]{1,0:T(8,128)(2,1)} %param.4), channel_id=1, replica_groups=mesh['dp'=4,'mx'=4,'my'=2] {'my'}, dimensions={1}, use_global_device_ids=true | all-gather | bytes 1179648 | tf_op jit(solution)/shard_map/all_gather | solution.py:14
  20.2 11.2 %all_gather.7 = bf16[256,1536]{1,0:T(8,128)(2,1)S(1)} all-gather(bf16[256,768]{1,0:T(8,128)(2,1)} %param.5), channel_id=1, replica_groups=mesh['dp'=4,'mx'=4,'my'=2] {'my'}, dimensions={1}, use_global_device_ids=true | all-gather | bytes 1179648 | tf_op jit(solution)/shard_map/all_gather | solution.py:21
  31.4 10.1 %convolution_convert_fusion.2 = bf16[256,6144]{1,0:T(8,128)(2,1)} fusion(bf16[256,1536]{1,0:T(8,128)(2,1)S(1)} %all_gather.7, bf16[6144,1536]{1,0:T(8,128)(2,1)} %param.7), kind=kOutput, calls=%fused_computation.8 | convolution fusion | flops 4833411072 | bytes 22806528 | tf_op jit(solution)/shard_map/dot_general | solution.py:22
  41.5 12.8 %convolution_convert_fusion.3 = bf16[256,6144]{1,0:T(8,128)(2,1)} fusion(bf16[256,1536]{1,0:T(8,128)(2,1)S(1)} %all_gather.6, bf16[1536,6144]{1,0:T(8,128)(2,1)} %param.6), kind=kOutput, calls=%fused_computation.9 | convolution fusion | flops 4833411072 | bytes 22806528 | tf_op jit(solution)/shard_map/dot_general | solution.py:15
  54.3 0.0 all-reduce.3.cloned.1.call-update
  54.3 0.0 reduce-scatter.9.cloned.1.call-start
  54.4 224.4 %all-reduce.3.cloned.1.call-done = (bf16[256,6144]{1,0:T(8,128)(2,1)}, bf16[256,6144]{1,0:T(8,128)(2,1)}) async-done(((bf16[256,6144]{1,0:T(8,128)(2,1)}, bf16[256,6144]{1,0:T(8,128)(2,1)}), (bf16[256,6144]{1,0:T(8,128)(2,1)}, bf16[256,6144]{1,0:T(8,128)(2,1)})) %all-reduce.3.cloned.1.call-update) | async-done | bytes 6291472 | tf_op jit(solution)/shard_map/psum | solution.py:16
  278.8 13.4 %fusion = bf16[1536,6144]{0,1:T(8,128)(2,1)} fusion(bf16[256,1536]{1,0:T(8,128)(2,1)S(1)} %all_gather.6, bf16[256,6144]{1,0:T(8,128)(2,1)} %get-tuple-element.8, bf16[256,6144]{1,0:T(8,128)(2,1)} %get-tuple-element.9), kind=kOutput, calls=%fused_computation.2 | convolution fusion | flops 4860149760 | bytes 25952256 | tf_op jit(solution)/shard_map/dot_general | solution.py:33
  292.2 0.0 reduce-scatter.9.cloned.1.call-update
  292.2 0.0 reduce-scatter.7.cloned.1.call-start
  292.3 14.7 %convolution_convert_fusion.4 = bf16[256,1536]{1,0:T(8,128)(2,1)} fusion(bf16[1536,6144]{1,0:T(8,128)(2,1)} %param.6, bf16[256,6144]{1,0:T(8,128)(2,1)} %get-tuple-element.8, bf16[256,6144]{1,0:T(8,128)(2,1)} %get-tuple-element.9), kind=kOutput, calls=%fused_computation.19 | convolution fusion | flops 4851105792 | bytes 25952256 | tf_op jit(solution)/shard_map/dot_general | solution.py:27
  306.9 0.0 reduce-scatter.7.cloned.1.call-update
  306.9 0.2 reduce-scatter.5.cloned.1.call-start
  307.2 17.6 %convolution_convert_fusion.5 = bf16[256,1536]{1,0:T(8,128)(2,1)} fusion(bf16[6144,1536]{1,0:T(8,128)(2,1)} %param.7, bf16[256,6144]{1,0:T(8,128)(2,1)} %get-tuple-element.8), kind=kOutput, calls=%fused_computation.20 | convolution fusion | flops 4841668608 | bytes 22806528 | tf_op jit(solution)/shard_map/dot_general | solution.py:19
  324.8 0.0 reduce-scatter.5.cloned.1.call-update
  324.8 0.0 reduce-scatter.11.cloned.1.call-start
  324.9 10.8 %convolution_convert_fusion = bf16[6144,1536]{1,0:T(8,128)(2,1)} fusion(bf16[256,1536]{1,0:T(8,128)(2,1)S(1)} %all_gather.7, bf16[256,6144]{1,0:T(8,128)(2,1)} %get-tuple-element.8), kind=kOutput, calls=%fused_computation | convolution fusion | flops 4850712576 | bytes 22806528 | tf_op jit(solution)/shard_map/dot_general | solution.py:36
  335.7 0.0 reduce-scatter.11.cloned.1.call-update
  335.7 95.1 %reduce-scatter.9.cloned.1.call-done = bf16[1536,1536]{0,1:T(8,128)(2,1)} async-done(((bf16[1536,6144]{0,1:T(8,128)(2,1)}), bf16[1536,1536]{0,1:T(8,128)(2,1)}) %reduce-scatter.9.cloned.1.call-update) | async-done | bytes 4718608 | tf_op jit(solution)/shard_map/reduce_scatter | solution.py:39
  430.8 6.6 %copy.8 = bf16[1536,1536]{1,0:T(8,128)(2,1)} copy(bf16[1536,1536]{0,1:T(8,128)(2,1)} %reduce-scatter.9.cloned.1.call-done) | data formatting | bytes 9437184
  437.4 13.8 %reduce-scatter.7.cloned.1.call-done = bf16[256,768]{1,0:T(8,128)(2,1)} async-done(((bf16[256,1536]{1,0:T(8,128)(2,1)}), bf16[256,768]{1,0:T(8,128)(2,1)}) %reduce-scatter.7.cloned.1.call-update) | async-done | bytes 393232 | tf_op jit(solution)/shard_map/reduce_scatter | solution.py:30
  451.2 20.1 %reduce-scatter.5.cloned.1.call-done = bf16[256,768]{1,0:T(8,128)(2,1)} async-done(((bf16[256,1536]{1,0:T(8,128)(2,1)}), bf16[256,768]{1,0:T(8,128)(2,1)}) %reduce-scatter.5.cloned.1.call-update) | async-done | bytes 393232 | tf_op jit(solution)/shard_map/reduce_scatter | solution.py:20
  471.3 142.7 %reduce-scatter.11.cloned.1.call-done = bf16[1536,1536]{1,0:T(8,128)(2,1)} async-done(((bf16[6144,1536]{1,0:T(8,128)(2,1)}), bf16[1536,1536]{1,0:T(8,128)(2,1)}) %reduce-scatter.11.cloned.1.call-update) | async-done | bytes 4718608 | tf_op jit(solution)/shard_map/reduce_scatter | solution.py:42
Async XLA Ops:
  7.2 271.6 %all-reduce.3.cloned.1.call-start = ((), (), s32[]{:S(2)}) async-start(), calls=%async_computation.8 | async-start | bytes 12582912 | tf_op jit(solution)/shard_map/psum | solution.py:16
  54.3 376.5 %reduce-scatter.9.cloned.1.call-start = ((), (), s32[]{:S(2)}) async-start(), calls=%async_computation.6 | async-start | bytes 23592960 | tf_op jit(solution)/shard_map/reduce_scatter | solution.py:39
  292.2 159.0 %reduce-scatter.7.cloned.1.call-start = ((), (), s32[]{:S(2)}) async-start(), calls=%async_computation.5 | async-start | bytes 1179648 | tf_op jit(solution)/shard_map/reduce_scatter | solution.py:30
  306.9 164.4 %reduce-scatter.5.cloned.1.call-start = ((), (), s32[]{:S(2)}) async-start(), calls=%async_computation.4 | async-start | bytes 1179648 | tf_op jit(solution)/shard_map/reduce_scatter | solution.py:20
  324.8 289.2 %reduce-scatter.11.cloned.1.call-start = ((), (), s32[]{:S(2)}) async-start(), calls=%async_computation.7 | async-start | bytes 23592960 | tf_op jit(solution)/shard_map/reduce_scatter | solution.py:42
Sparse Core Ops, SparseCore 0:
  54.4 224.3 all-reduce.2
  292.3 138.4 reduce-scatter.8
  433.7 17.4 reduce-scatter.6
  453.9 17.4 reduce-scatter.4
  474.5 139.4 reduce-scatter.10
where the time goes:
time: 621 us
  waiting for transfers between devices  496 us (80%)
  matrix products  79.3 us (13%)
  blocking collectives  24.2 us (4%)
  between operations  13.8 us (2%)
  local copies, waits for them, and re-layouts  6.61 us (1%)
    psum x1, waiting for transfers between devices, per_device(): lax.psum(hidden_part.astype(jnp.bfloat16), 'mx').astype(jnp.float32)  224 us
    reduce_scatter x1, waiting for transfers between devices, per_device(): lax.psum_scatter(out_term.astype(jnp.bfloat16), 'dp', scatter_dimension=0...  143 us
    reduce_scatter x1, waiting for transfers between devices, per_device(): lax.psum_scatter(in_part.astype(jnp.bfloat16), 'dp', scatter_dimension=1,...  95.1 us
    reduce_scatter x1, waiting for transfers between devices, per_device(): lax.psum_scatter(out_part.astype(jnp.bfloat16), 'my', scatter_dimension=1...  20.1 us
    dot_general x1, matrix products, per_device(): out_part = jnp.dot(active, w_out, preferred_element_type=jnp.float32)  17.6 us
    dot_general x1, matrix products, per_device(): lax.dot_general(hidden_grad, w_in, (((1,), (1,)), ((), ())), preferred_el...  14.7 us
    reduce_scatter x1, waiting for transfers between devices, per_device(): lax.psum_scatter(input_part.astype(jnp.bfloat16), 'my', scatter_dimension...  13.8 us
    dot_general x1, matrix products, per_device(): lax.dot_general(columns, hidden_grad, (((0,), (0,)), ((), ())), preferred...  13.4 us
  transfers between devices with their start and end apart: 5, of which 5 were waited for; matrix products, arithmetic and copies ran while one was open for 8% of the time, Pallas kernels for 0%

commit v1 on v0

v1 whole, which is shorter than its diff:
```python
import jax
import jax.numpy as jnp
from jax import lax
from jax.sharding import PartitionSpec as P


def gelu_parts(hidden):
    cdf = 0.5 * (1.0 + lax.erf(hidden * 0.7071067811865476))
    density = jnp.exp(-0.5 * hidden * hidden) * 0.3989422804014327
    return (hidden * cdf, cdf + hidden * density)


def mm(a, b, ca, cb):
    return lax.dot_general(
        a, b, (((ca,), (cb,)), ((), ())), preferred_element_type=jnp.float32
    ).astype(jnp.bfloat16)


def per_device(tokens, cotangent, w_in, w_out):
    n_dp = lax.axis_size("dp")
    width = w_in.shape[1] // n_dp
    start = lax.axis_index("dp") * width
    win = lax.dynamic_slice_in_dim(w_in, start, width, 1)
    wout = lax.dynamic_slice_in_dim(w_out, start, width, 0)

    def gather(x):
        x = lax.all_gather(x, "my", axis=1, tiled=True)
        return lax.all_gather(x, "dp", axis=0, tiled=True)

    def scatter(x):
        x = lax.psum_scatter(x, "dp", scatter_dimension=0, tiled=True)
        return lax.psum_scatter(x, "my", scatter_dimension=1, tiled=True)

    toks = gather(tokens)
    cots = gather(cotangent)
    hidden = lax.psum_scatter(mm(toks, win, 1, 0), "mx", scatter_dimension=0, tiled=True)
    act_grad = lax.psum_scatter(mm(cots, wout, 1, 1), "mx", scatter_dimension=0, tiled=True)
    act_full, slope = gelu_parts(hidden.astype(jnp.float32))
    active = act_full.astype(jnp.bfloat16)
    hidden_grad = (act_grad.astype(jnp.float32) * slope).astype(jnp.bfloat16)
    active = lax.all_gather(active, "mx", axis=0, tiled=True)
    hidden_grad = lax.all_gather(hidden_grad, "mx", axis=0, tiled=True)
    output = scatter(mm(active, wout, 1, 0))
    input_grad = scatter(mm(hidden_grad, win, 1, 1))
    w_out_grad = mm(active, cots, 0, 0)
    w_in_grad = mm(toks, hidden_grad, 0, 0)
    return (output, input_grad, w_in_grad, w_out_grad)


def solution(mesh):
    in_specs = (P("dp", ("mx", "my")), P("dp", ("mx", "my")), P("mx", "my"), P("my", "mx"))
    out_specs = (
        P("dp", ("mx", "my")),
        P("dp", ("mx", "my")),
        P("mx", ("my", "dp")),
        P(("my", "dp"), "mx"),
    )
    return jax.shard_map(
        per_device, mesh=mesh, in_specs=in_specs, out_specs=out_specs, check_vma=False
    )
```

time: 621 us -> 466 us (0.75)
  waiting for transfers between devices: 496 us -> 361 us
  matrix products: 79.3 us -> 54.3 us
    psum x1 -> x0, waiting for transfers between devices: 224 us -> none  [per_device(): lax.psum(hidden_part.astype(jnp.bfloat16), 'mx').astype(jnp.float32)]
    all_gather x0 -> x4, waiting for transfers between devices: none -> 156 us  [the longest x1 63 us: per_device(): active = lax.all_gather(active, 'mx', axis=0, tiled=True)]
    reduce_scatter x4 -> x6, waiting for transfers between devices: 272 us -> 204 us  [the longest x2 70.9 us: scatter(): x = lax.psum_scatter(x, 'dp', scatter_dimension=0, tiled=True)]
    dot_general x6, matrix products: 79.3 us -> 54.3 us  [mm(): lax.dot_general(a, b, (((ca,), (cb,)), ((), ())), preferred_element_type=...]
  transfers between devices with their start and end apart: 5 -> 10, of which waited for: 5 -> 9; matrix products, arithmetic and copies ran while one was open for 8% -> 13% of each run, Pallas kernels for 0% -> 0%
where the time goes in v1:
time: 466 us
  waiting for transfers between devices  361 us (77%)
  matrix products  54.3 us (12%)
  blocking collectives  26.1 us (6%)
  between operations  14.2 us (3%)
  local copies, waits for them, and re-layouts  6.77 us (1%)
    reduce_scatter x2, waiting for transfers between devices, scatter(): x = lax.psum_scatter(x, 'dp', scatter_dimension=0, tiled=True)  70.9 us
    reduce_scatter x1, waiting for transfers between devices, per_device(): lax.psum_scatter(mm(toks, win, 1, 0), 'mx', scatter_dimension=0, tiled=True)  63 us
    all_gather x1, waiting for transfers between devices, per_device(): active = lax.all_gather(active, 'mx', axis=0, tiled=True)  63 us
    dot_general x6, matrix products, mm(): lax.dot_general(a, b, (((ca,), (cb,)), ((), ())), preferred_element_type=...  54.3 us
    all_gather x1, waiting for transfers between devices, per_device(): hidden_grad = lax.all_gather(hidden_grad, 'mx', axis=0, tiled=True)  54.3 us
    reduce_scatter x1, waiting for transfers between devices, per_device(): lax.psum_scatter(mm(cots, wout, 1, 1), 'mx', scatter_dimension=0, tiled=T...  53.8 us
    all_gather x2, waiting for transfers between devices, gather(): return lax.all_gather(x, 'dp', axis=0, tiled=True)  38.3 us
    all_gather x2, blocking collectives, gather(): x = lax.all_gather(x, 'my', axis=1, tiled=True)  26.1 us
  transfers between devices with their start and end apart: 10, of which 9 were waited for; matrix products, arithmetic and copies ran while one was open for 13% of the time, Pallas kernels for 0%

profile of v1, /device:TPU:0, one launch (start us, length us, event | category | flops | bytes accessed | tf_op | source)
XLA Modules:
  0.0 465.8 jit_solution(361520226639755532)
XLA Ops:
  7.2 14.8 %all_gather.21 = bf16[256,1536]{1,0:T(8,128)(2,1)} all-gather(bf16[256,768]{1,0:T(8,128)(2,1)} %param.5), channel_id=1, replica_groups=mesh['dp'=4,'mx'=4,'my'=2] {'my'}, dimensions={1}, use_global_device_ids=true | all-gather | bytes 1179648 | tf_op jit(solution)/shard_map/all_gather | solution.py:27
  22.0 0.0 all-gather.5.cloned.1.call-start
  22.1 11.3 %all_gather.18 = bf16[256,1536]{1,0:T(8,128)(2,1)} all-gather(bf16[256,768]{1,0:T(8,128)(2,1)} %param.4), channel_id=1, replica_groups=mesh['dp'=4,'mx'=4,'my'=2] {'my'}, dimensions={1}, use_global_device_ids=true | all-gather | bytes 1179648 | tf_op jit(solution)/shard_map/all_gather | solution.py:27
  33.4 17.6 %all-gather.9.cloned.1.call-done = bf16[1024,1536]{1,0:T(8,128)(2,1)} async-done(((bf16[256,1536]{1,0:T(8,128)(2,1)}), bf16[1024,1536]{1,0:T(8,128)(2,1)}) %all-gather.9.cloned.1.call-update) | async-done | bytes 3145744 | tf_op jit(solution)/shard_map/all_gather | solution.py:28
  51.0 9.3 %fusion.21 = bf16[1024,1536]{0,1:T(8,128)(2,1)} fusion(bf16[1024,1536]{1,0:T(8,128)(2,1)} %all-gather.9.cloned.1.call-done, bf16[6144,1536]{1,0:T(8,128)(2,1)} %param.7, s32[]{:T(128)S(6)} %select_n.4), kind=kOutput, calls=%fused_computation.15 | convolution fusion | flops 4833411072 | bytes 11010052 | tf_op jit(solution)/shard_map/dot_general | solution.py:14
  60.3 0.0 reduce-scatter.7.cloned.1.call-start
  60.4 20.8 %all-gather.5.cloned.1.call-done = bf16[1024,1536]{1,0:T(8,128)(2,1)} async-done(((bf16[256,1536]{1,0:T(8,128)(2,1)}), bf16[1024,1536]{1,0:T(8,128)(2,1)}) %all-gather.5.cloned.1.call-update) | async-done | bytes 3145744 | tf_op jit(solution)/shard_map/all_gather | solution.py:28
  81.1 9.3 %fusion.24 = bf16[1024,1536]{0,1:T(8,128)(2,1)} fusion(bf16[1024,1536]{1,0:T(8,128)(2,1)} %all-gather.5.cloned.1.call-done, bf16[1536,6144]{1,0:T(8,128)(2,1)} %param.6, s32[]{:T(128)S(6)} %select_n.4), kind=kOutput, calls=%fused_computation.16 | convolution fusion | flops 4833411072 | bytes 11010052 | tf_op jit(solution)/shard_map/dot_general | solution.py:14
  90.5 0.0 all-gather.7.cloned.1.call-start
  90.5 53.8 %reduce-scatter.13.cloned.1.call-done = bf16[256,1536]{0,1:T(8,128)(2,1)} async-done(((bf16[1024,1536]{0,1:T(8,128)(2,1)}), bf16[256,1536]{0,1:T(8,128)(2,1)}) %reduce-scatter.13.cloned.1.call-update) | async-done | bytes 786448 | tf_op jit(solution)/shard_map/reduce_scatter | solution.py:37
  144.3 63.0 %reduce-scatter.7.cloned.1.call-done = bf16[256,1536]{0,1:T(8,128)(2,1)} async-done(((bf16[1024,1536]{0,1:T(8,128)(2,1)}), bf16[256,1536]{0,1:T(8,128)(2,1)}) %reduce-scatter.7.cloned.1.call-update) | async-done | bytes 786448 | tf_op jit(solution)/shard_map/reduce_scatter | solution.py:36
  207.4 3.3 fusion.35
  210.7 0.5 all-gather.11.cloned.1.call-update
  211.3 63.0 %all-gather.7.cloned.1.call-done = bf16[1024,1536]{0,1:T(8,128)(2,1)} async-done(((bf16[256,1536]{0,1:T(8,128)(2,1)}), bf16[1024,1536]{0,1:T(8,128)(2,1)}) %all-gather.7.cloned.1.call-update) | async-done | bytes 3145744 | tf_op jit(solution)/shard_map/all_gather | solution.py:41
  274.3 9.3 %fusion.15 = bf16[1024,1536]{1,0:T(8,128)(2,1)} fusion(bf16[1024,1536]{0,1:T(8,128)(2,1)} %all-gather.7.cloned.1.call-done, bf16[6144,1536]{1,0:T(8,128)(2,1)} %param.7, s32[]{:T(128)S(6)} %select_n.4), kind=kOutput, calls=%fused_computation.13 | convolution fusion | flops 4833411072 | bytes 11010052 | tf_op jit(solution)/shard_map/dot_general | solution.py:14
  283.6 54.3 %all-gather.11.cloned.1.call-done = bf16[1024,1536]{0,1:T(8,128)(2,1)} async-done(((bf16[256,1536]{0,1:T(8,128)(2,1)}), bf16[1024,1536]{0,1:T(8,128)(2,1)}) %all-gather.11.cloned.1.call-update) | async-done | bytes 3145744 | tf_op jit(solution)/shard_map/all_gather | solution.py:42
  337.9 9.3 %fusion.12 = bf16[1024,1536]{1,0:T(8,128)(2,1)} fusion(bf16[1024,1536]{0,1:T(8,128)(2,1)} %all-gather.11.cloned.1.call-done, bf16[1536,6144]{1,0:T(8,128)(2,1)} %param.6, s32[]{:T(128)S(6)} %select_n.4), kind=kOutput, calls=%fused_computation.12 | convolution fusion | flops 4833411072 | bytes 11010052 | tf_op jit(solution)/shard_map/dot_general | solution.py:14
  347.3 29.9 %reduce-scatter.9.cloned.1.call-done = bf16[256,1536]{1,0:T(8,128)(2,1)} async-done(((bf16[1024,1536]{1,0:T(8,128)(2,1)}), bf16[256,1536]{1,0:T(8,128)(2,1)}) %reduce-scatter.9.cloned.1.call-update) | async-done | bytes 786448 | tf_op jit(solution)/shard_map/reduce_scatter | solution.py:31
  377.2 0.2 reduce-scatter.17.cloned.1.call-start
  377.5 41.0 %reduce-scatter.15.cloned.1.call-done = bf16[256,1536]{1,0:T(8,128)(2,1)} async-done(((bf16[1024,1536]{1,0:T(8,128)(2,1)}), bf16[256,1536]{1,0:T(8,128)(2,1)}) %reduce-scatter.15.cloned.1.call-update) | async-done | bytes 786448 | tf_op jit(solution)/shard_map/reduce_scatter | solution.py:31
  418.5 8.6 %fusion = bf16[1536,1536]{0,1:T(8,128)(2,1)} fusion(bf16[1024,1536]{0,1:T(8,128)(2,1)} %all-gather.11.cloned.1.call-done, bf16[1024,1536]{1,0:T(8,128)(2,1)S(1)} %copy-done.1), kind=kOutput, calls=%fused_computation.2 | convolution fusion | flops 4834197504 | bytes 11010048 | tf_op jit(solution)/shard_map/dot_general | solution.py:14
  427.1 6.8 %copy.8 = bf16[1536,1536]{1,0:T(8,128)(2,1)} copy(bf16[1536,1536]{0,1:T(8,128)(2,1)} %fusion) | data formatting | bytes 9437184
  433.8 8.6 %convolution_convert_fusion = bf16[1536,1536]{1,0:T(8,128)(2,1)} fusion(bf16[1024,1536]{0,1:T(8,128)(2,1)} %all-gather.7.cloned.1.call-done, bf16[1024,1536]{1,0:T(8,128)(2,1)S(1)} %copy-done), kind=kOutput, calls=%fused_computation | convolution fusion | flops 4834197504 | bytes 11010048 | tf_op jit(solution)/shard_map/dot_general | solution.py:14
  442.5 16.5 %reduce-scatter.17.cloned.1.call-done = bf16[256,768]{1,0:T(8,128)(2,1)} async-done(((bf16[256,1536]{1,0:T(8,128)(2,1)}), bf16[256,768]{1,0:T(8,128)(2,1)}) %reduce-scatter.17.cloned.1.call-update) | async-done | bytes 393232 | tf_op jit(solution)/shard_map/reduce_scatter | solution.py:32
  (20 shorter events, 0.4 us)
Async XLA Ops:
  7.2 43.8 %all-gather.9.cloned.1.call-start = ((), (), s32[]{:S(2)}) async-start(), calls=%async_computation.11 | async-start | bytes 3932160 | tf_op jit(solution)/shard_map/all_gather | solution.py:28
  22.0 59.1 %all-gather.5.cloned.1.call-start = ((), (), s32[]{:S(2)}) async-start(), calls=%async_computation.6 | async-start | bytes 3932160 | tf_op jit(solution)/shard_map/all_gather | solution.py:28
  33.4 110.9 %reduce-scatter.13.cloned.1.call-start = ((), (), s32[]{:S(2)}) async-start(), calls=%async_computation.12 | async-start | bytes 3932160 | tf_op jit(solution)/shard_map/reduce_scatter | solution.py:37
  60.3 147.0 %reduce-scatter.7.cloned.1.call-start = ((), (), s32[]{:S(2)}) async-start(), calls=%async_computation.7 | async-start | bytes 3932160 | tf_op jit(solution)/shard_map/reduce_scatter | solution.py:36
  90.5 183.8 %all-gather.7.cloned.1.call-start = ((), (), s32[]{:S(2)}) async-start(), calls=%async_computation.8 | async-start | bytes 3932160 | tf_op jit(solution)/shard_map/all_gather | solution.py:41
  210.7 127.2 %all-gather.11.cloned.1.call-start = ((), (), s32[]{:S(2)}) async-start(), calls=%async_computation.13 | async-start | bytes 3932160 | tf_op jit(solution)/shard_map/all_gather | solution.py:42
  211.3 165.9 %reduce-scatter.9.cloned.1.call-start = ((), (), s32[]{:S(2)}) async-start(), calls=%async_computation.9 | async-start | bytes 3932160 | tf_op jit(solution)/shard_map/reduce_scatter | solution.py:31
  283.6 134.9 %reduce-scatter.15.cloned.1.call-start = ((), (), s32[]{:S(2)}) async-start(), calls=%async_computation.14 | async-start | bytes 3932160 | tf_op jit(solution)/shard_map/reduce_scatter | solution.py:31
  347.2 71.3 %copy-start.1 = (bf16[1024,1536]{1,0:T(8,128)(2,1)S(1)}, bf16[1024,1536]{1,0:T(8,128)(2,1)}, u32[]{:S(2)}) copy-start(bf16[1024,1536]{1,0:T(8,128)(2,1)} %all-gather.5.cloned.1.call-done) | copy-start | bytes 9437188
  347.3 95.2 %reduce-scatter.11.cloned.1.call-start = ((), (), s32[]{:S(2)}) async-start(), calls=%async_computation.10 | async-start | bytes 1179648 | tf_op jit(solution)/shard_map/reduce_scatter | solution.py:32
  377.2 81.7 %reduce-scatter.17.cloned.1.call-start = ((), (), s32[]{:S(2)}) async-start(), calls=%async_computation.15 | async-start | bytes 1179648 | tf_op jit(solution)/shard_map/reduce_scatter | solution.py:32
  427.1 6.8 %copy-start = (bf16[1024,1536]{1,0:T(8,128)(2,1)S(1)}, bf16[1024,1536]{1,0:T(8,128)(2,1)}, u32[]{:S(2)}) copy-start(bf16[1024,1536]{1,0:T(8,128)(2,1)} %all-gather.9.cloned.1.call-done) | copy-start | bytes 9437188
Sparse Core Ops, SparseCore 0:
  22.1 28.8 all-gather.8
  52.6 28.5 all-gather.4
  84.0 60.2 reduce-scatter.12
  147.0 60.2 reduce-scatter.6
  210.8 63.4 all-gather.6
  276.3 61.5 all-gather.10
  341.0 36.1 reduce-scatter.8
  380.5 37.9 reduce-scatter.14
  421.3 17.4 reduce-scatter.10
  441.5 17.4 reduce-scatter.16

commit v2 on v1

--- a/solution.py
+++ b/solution.py
@@ -1,6 +1,10 @@
+import functools
+
 import jax
 import jax.numpy as jnp
 from jax import lax
+from jax.experimental import pallas as pl
+from jax.experimental.pallas import tpu as pltpu
 from jax.sharding import PartitionSpec as P
 
 
@@ -16,8 +20,279 @@
     ).astype(jnp.bfloat16)
 
 
+MESH = pl.DeviceIdType.MESH
+TILE = 256
+SKEW = 2
+
+
+def dot(a, b, ca, cb):
+    return lax.dot_general(a, b, (((ca,), (cb,)), ((), ())), preferred_element_type=jnp.float32)
+
+
+def kernel(
+    n, tok_ref, cot_ref, win_hbm, wout_hbm, out_ref, toks_hbm, cots_hbm, acts_hbm,
+    win, wout, toks, cots, sums, acts, parts, landed,
+    local_sem, gat_send, gat_recv, rs_send, rs_recv, ag_send, ag_recv, out_send, out_recv,
+):
+    dp, z, my = lax.axis_index("dp"), lax.axis_index("mx"), lax.axis_index("my")
+    x, c = dp // 2, dp % 2
+    rows, width = tok_ref.shape
+    hidden = win.shape[1]
+    half = hidden // 2
+    per_half = half // TILE
+    steps = 4 * per_half
+    lag = (n - 1) * SKEW
+
+    def block_of(j):
+        return ((x + ((j + 1) // 2) % 2) % 2) * 2 + (c + j // 2) % 2
+
+    def row_slice(t):
+        return pl.ds(pl.multiple_of(t * rows, rows), rows)
+
+    def col_slice(m):
+        return pl.ds(pl.multiple_of(m * width, width), width)
+
+    peers = []
+    for co, xo, yo in ((0, 0, 1), (0, 1, 0), (0, 1, 1), (1, 1, 0), (1, 1, 1), (1, 0, 0), (1, 0, 1)):
+        peers.append((((x + xo) % 2) * 2 + (c + co) % 2, (my + yo) % 2))
+
+    cut = pl.ds(pl.multiple_of(dp * hidden, hidden), hidden)
+    loads = [
+        pltpu.make_async_copy(win_hbm.at[:, cut], win, local_sem.at[0]),
+        pltpu.make_async_copy(wout_hbm.at[cut, :], wout, local_sem.at[1]),
+        pltpu.make_async_copy(tok_ref, toks.at[row_slice(dp), col_slice(my)], local_sem.at[2]),
+        pltpu.make_async_copy(cot_ref, cots.at[row_slice(dp), col_slice(my)], local_sem.at[3]),
+    ]
+    for load in loads:
+        load.start()
+
+    barrier = pltpu.get_barrier_semaphore()
+    for pd, pm in peers:
+        pl.semaphore_signal(barrier, inc=1, device_id=(pd, z, pm), device_id_type=MESH)
+
+    @pl.when(z > 0)
+    def _():
+        pl.semaphore_signal(barrier, inc=1, device_id=(dp, z - 1, my), device_id_type=MESH)
+
+    @pl.when(z < n - 1)
+    def _():
+        pl.semaphore_signal(barrier, inc=1, device_id=(dp, z + 1, my), device_id_type=MESH)
+
+    pl.semaphore_wait(barrier, 7 + jnp.where(z > 0, 1, 0) + jnp.where(z < n - 1, 1, 0))
+
+    def gather_copy(k, src_ref, dst, source, target):
+        return pltpu.make_async_remote_copy(
+            src_ref=src_ref,
+            dst_ref=dst.at[row_slice(source[0]), col_slice(source[1])],
+            send_sem=gat_send.at[k, target[0] * 2 + target[1]],
+            recv_sem=gat_recv.at[k, source[0] * 2 + source[1]],
+            device_id=(target[0], z, target[1]),
+            device_id_type=MESH,
+        )
+
+    for peer in peers:
+        gather_copy(0, tok_ref, toks, (dp, my), peer).start()
+        gather_copy(1, cot_ref, cots, (dp, my), peer).start()
+
+    def tile_of(d, idx):
+        t = block_of(idx // per_half)
+        first = pl.multiple_of(d * half + (idx % per_half) * TILE, TILE)
+        return row_slice(t), pl.ds(first, TILE)
+
+    def chain_copy(buf, sends, recvs, d, idx, target):
+        r, f = tile_of(d, idx)
+        return pltpu.make_async_remote_copy(
+            src_ref=buf.at[:, r, f],
+            dst_ref=buf.at[:, r, f],
+            send_sem=sends.at[d, idx],
+            recv_sem=recvs.at[d, idx],
+            device_id=(dp, target, my),
+            device_id_type=MESH,
+        )
+
+    def out_copy(t, m, source, target):
+        return pltpu.make_async_remote_copy(
+            src_ref=parts.at[:, row_slice(t), col_slice(m)],
+            dst_ref=landed.at[:, source[0] * 2 + source[1]],
+            send_sem=out_send.at[t * 2 + m],
+            recv_sem=out_recv.at[source[0] * 2 + source[1]],
+            device_id=(target[0], z, target[1]),
+            device_id_type=MESH,
+        )
+
+    for load in loads:
+        load.wait()
+
+    nearest = jnp.minimum(z, n - 1 - z)
+
+    @pl.loop(0, steps + 2 * lag)
+    def _(s):
+        lead = s - nearest * SKEW
+
+        @pl.when((lead >= 0) & (lead < steps) & (lead % per_half == 0))
+        def _():
+            t = block_of(lead // per_half)
+            for m in range(2):
+                @pl.when((t != dp) | (my != m))
+                def _():
+                    gather_copy(0, tok_ref, toks, (t, m), (dp, my)).wait_recv()
+                    gather_copy(1, cot_ref, cots, (t, m), (dp, my)).wait_recv()
+
+        for d in range(2):
+            pos = z if d == 0 else n - 1 - z
+            ahead = z + 1 if d == 0 else z - 1
+            behind = z - 1 if d == 0 else z + 1
+            idx = s - pos * SKEW
+
+            @pl.when((idx >= 0) & (idx < steps))
+            def _():
+                r, f = tile_of(d, idx)
+                h = dot(toks[r, :], win[:, f], 1, 0)
+                a = dot(cots[r, :], wout[f, :], 1, 1)
+
+                @pl.when(pos == 0)
+                def _():
+                    sums[0, r, f] = h.astype(jnp.bfloat16)
+                    sums[1, r, f] = a.astype(jnp.bfloat16)
+                    chain_copy(sums, rs_send, rs_recv, d, idx, ahead).start()
+
+                @pl.when((pos > 0) & (pos < n - 1))
+                def _():
+                    chain_copy(sums, rs_send, rs_recv, d, idx, ahead).wait_recv()
+                    sums[0, r, f] = (sums[0, r, f].astype(jnp.float32) + h).astype(jnp.bfloat16)
+                    sums[1, r, f] = (sums[1, r, f].astype(jnp.float32) + a).astype(jnp.bfloat16)
+                    chain_copy(sums, rs_send, rs_recv, d, idx, ahead).start()
+
+                @pl.when(pos == n - 1)
+                def _():
+                    chain_copy(sums, rs_send, rs_recv, d, idx, behind).wait_recv()
+                    hs = sums[0, r, f].astype(jnp.float32) + h
+                    grad = sums[1, r, f].astype(jnp.float32) + a
+                    act_full, slope = gelu_parts(hs)
+                    acts[0, r, f] = act_full.astype(jnp.bfloat16)
+                    acts[1, r, f] = (grad * slope).astype(jnp.bfloat16)
+                    chain_copy(acts, ag_send, ag_recv, d, idx, behind).start()
+
+            back = s - lag - (n - 1 - pos) * SKEW
+
+            @pl.when((back >= 0) & (back < steps) & (pos < n - 1))
+            def _():
+                chain_copy(acts, ag_send, ag_recv, d, back, ahead).wait_recv()
+
+                @pl.when(pos > 0)
+                def _():
+                    chain_copy(acts, ag_send, ag_recv, d, back, behind).start()
+
+        done = s - 2 * lag
+
+        @pl.when((done >= 0) & (done % per_half == per_half - 1))
+        def _():
+            t = block_of(done // per_half)
+            r = row_slice(t)
+            parts[0, r, :] = dot(acts[0, r, :], wout[...], 1, 0).astype(jnp.bfloat16)
+            parts[1, r, :] = dot(acts[1, r, :], win[...], 1, 1).astype(jnp.bfloat16)
+            for m in range(2):
+                @pl.when((t != dp) | (my != m))
+                def _():
+                    out_copy(t, m, (dp, my), (t, m)).start()
+
+    stores = [
+        pltpu.make_async_copy(toks, toks_hbm, local_sem.at[0]),
+        pltpu.make_async_copy(cots, cots_hbm, local_sem.at[1]),
+        pltpu.make_async_copy(acts, acts_hbm, local_sem.at[2]),
+    ]
+    for store in stores:
+        store.start()
+
+    for d in range(2):
+        pos = z if d == 0 else n - 1 - z
+
+        @pl.loop(0, steps)
+        def _(idx):
+            other = jnp.where(z == 0, 1, z - 1)
+
+            @pl.when(pos < n - 1)
+            def _():
+                chain_copy(sums, rs_send, rs_recv, d, idx, other).wait_send()
+
+            @pl.when(pos > 0)
+            def _():
+                chain_copy(acts, ag_send, ag_recv, d, idx, other).wait_send()
+
+    for peer in peers:
+        gather_copy(0, tok_ref, toks, (dp, my), peer).wait_send()
+        gather_copy(1, cot_ref, cots, (dp, my), peer).wait_send()
+
+    out_ref[...] = parts[:, row_slice(dp), col_slice(my)].astype(jnp.float32)
+    for peer in peers:
+        out_copy(dp, my, peer, peer).wait_recv()
+        out_ref[...] += landed[:, peer[0] * 2 + peer[1]].astype(jnp.float32)
+    for peer in peers:
+        out_copy(peer[0], peer[1], (dp, my), peer).wait_send()
+    for store in stores:
+        store.wait()
+
+
+def fused(tokens, cotangent, w_in, w_out):
+    n = lax.axis_size("mx")
+    rows, width = tokens.shape
+    hidden = w_in.shape[1] // 4
+    deep = w_in.shape[0]
+    bf16 = jnp.bfloat16
+    steps = 4 * (hidden // 2 // TILE)
+    vmem = pl.BlockSpec(memory_space=pltpu.VMEM)
+    hbm = pl.BlockSpec(memory_space=pl.ANY)
+    dma = pltpu.SemaphoreType.DMA
+    outs, toks, cots, acts = pl.pallas_call(
+        functools.partial(kernel, n),
+        out_shape=(
+            jax.ShapeDtypeStruct((2, rows, width), jnp.float32),
+            jax.ShapeDtypeStruct((4 * rows, deep), bf16),
+            jax.ShapeDtypeStruct((4 * rows, deep), bf16),
+            jax.ShapeDtypeStruct((2, 4 * rows, hidden), bf16),
+        ),
+        in_specs=[vmem, vmem, hbm, hbm],
+        out_specs=(vmem, hbm, hbm, hbm),
+        scratch_shapes=[
+            pltpu.VMEM((deep, hidden), bf16),
+            pltpu.VMEM((hidden, deep), bf16),
+            pltpu.VMEM((4 * rows, deep), bf16),
+            pltpu.VMEM((4 * rows, deep), bf16),
+            pltpu.VMEM((2, 4 * rows, hidden), bf16),
+            pltpu.VMEM((2, 4 * rows, hidden), bf16),
+            pltpu.VMEM((2, 4 * rows, deep), bf16),
+            pltpu.VMEM((2, 8, rows, width), bf16),
+            dma((4,)),
+            dma((2, 8)),
+            dma((2, 8)),
+            dma((2, steps)),
+            dma((2, steps)),
+            dma((2, steps)),
+            dma((2, steps)),
+            dma((8,)),
+            dma((8,)),
+        ],
+        compiler_params=pltpu.CompilerParams(
+            collective_id=0, has_side_effects=True, vmem_limit_bytes=60 * 2**20
+        ),
+        cost_estimate=pl.CostEstimate(
+            flops=16 * rows * hidden * deep * 2, bytes_accessed=4 * hidden * deep, transcendentals=0
+        ),
+    )(tokens, cotangent, w_in, w_out)
+    return (
+        outs[0].astype(bf16),
+        outs[1].astype(bf16),
+        mm(toks, acts[1], 0, 0),
+        mm(acts[0], cots, 0, 0),
+    )
+
+
 def per_device(tokens, cotangent, w_in, w_out):
     n_dp = lax.axis_size("dp")
+    aligned = tokens.shape[0] % 16 == 0 and tokens.shape[1] % 128 == 0
+    aligned = aligned and w_in.shape[1] % (8 * TILE) == 0
+    if n_dp == 4 and lax.axis_size("my") == 2 and lax.axis_size("mx") > 1 and aligned:
+        return fused(tokens, cotangent, w_in, w_out)
     width = w_in.shape[1] // n_dp
     start = lax.axis_index("dp") * width
     win = lax.dynamic_slice_in_dim(w_in, start, width, 1)

time: 466 us -> 268 us (0.58)
  waiting for transfers between devices: 361 us -> 0 us
  Pallas kernels: 0 us -> 249 us
  matrix products: 54.3 us -> 16.5 us
  blocking collectives: 26.1 us -> 0 us
  between operations: 14.2 us -> 0.66 us
  local copies, waits for them, and re-layouts: 6.77 us -> 0.94 us
    pallas_call x0 -> x1, Pallas kernels: none -> 249 us  [fused(): pl.pallas_call(functools.partial(kernel, n), out_shape=(jax.ShapeDtypeStr...]
    reduce_scatter x6 -> x0, waiting for transfers between devices: 204 us -> none  [the longest x2 70.9 us: scatter(): x = lax.psum_scatter(x, 'dp', scatter_dimension=0, tiled=True)]
    all_gather x4 -> x0, waiting for transfers between devices: 156 us -> none  [the longest x1 63 us: per_device(): active = lax.all_gather(active, 'mx', axis=0, tiled=True)]
    dot_general x6 -> x2, matrix products: 54.3 us -> 16.5 us  [mm(): lax.dot_general(a, b, (((ca,), (cb,)), ((), ())), preferred_element_type=...]
    all_gather x2 -> x0, blocking collectives: 26.1 us -> none  [gather(): x = lax.all_gather(x, 'my', axis=1, tiled=True)]
    unnamed x5 -> x6, local copies, waits for them, and re-layouts: 6.77 us -> 0.01 us
  transfers between devices with their start and end apart: 10 -> 0, of which waited for: 9 -> 0; matrix products, arithmetic and copies ran while one was open for 13% -> 0% of each run, Pallas kernels for 0% -> 0%
where the time goes in v2:
time: 268 us
  Pallas kernels  249 us (93%)
  matrix products  16.5 us (6%)
    pallas_call x1, Pallas kernels, fused(): pl.pallas_call(functools.partial(kernel, n), out_shape=(jax.ShapeDtypeStr...  249 us
    dot_general x2, matrix products, mm(): lax.dot_general(a, b, (((ca,), (cb,)), ((), ())), preferred_element_type=...  16.5 us

profile of v2, /device:TPU:0, one launch (start us, length us, event | category | flops | bytes accessed | tf_op | source)
XLA Modules:
  0.0 268.1 jit_solution(4324402057293757730)
XLA Ops:
  0.6 248.5 %shard_map.75 = (f32[2,256,768]{2,1,0:T(8,128)}, bf16[1024,1536]{1,0:T(8,128)(2,1)}, bf16[1024,1536]{1,0:T(8,128)(2,1)}, bf16[2,1024,1536]{2,1,0:T(8,128)(2,1)}) custom-call(bf16[256,768]{1,0:T(8,128)(2,1)} %tok_ref.1, bf16[256,768]{1,0:T(8,128)(2,1)} %cot_ref.1, bf16[1536,6144]{1,0:T(8,128)(2,1)} %win_hbm.1, bf16[6144,1536]{1,0:T(8,128)(2,1)} %wout_hbm.1), custom_call_target="tpu_custom_call" | custom-call | flops 19327352832 | bytes 9437184 | tf_op jit(solution)/shard_map/pallas_call | solution.py:246
  249.2 1.5 convert.4
  250.6 0.0 slice-start
  250.7 0.9 slice_bitcast_fusion
  251.6 0.0 slice-start.1
  251.6 0.0 copy-start
  251.6 9.7 %convolution_convert_fusion.1 = bf16[1536,1536]{1,0:T(8,128)(2,1)} fusion(bf16[1024,1536]{1,0:T(8,128)(2,1)} %get-tuple-element.9, bf16[2,1024,1536]{2,1,0:T(8,128)(2,1)} %get-tuple-element.10), kind=kOutput, calls=%fused_computation.1 | convolution fusion | flops 4834197504 | bytes 11010048 | tf_op jit(solution)/shard_map/dot_general | solution.py:18
  261.3 0.0 slice-done
  261.3 0.0 slice-done.1
  261.3 0.0 copy-done
  261.4 6.8 %convolution_convert_fusion = bf16[1536,1536]{1,0:T(8,128)(2,1)} fusion(bf16[1024,1536]{1,0:T(8,128)(2,1)S(1)} %copy-done, bf16[2,1024,1536]{2,1,0:T(8,128)(2,1)S(1)} %bitcast.13), kind=kOutput, calls=%fused_computation | convolution fusion | flops 4834197504 | bytes 11010048 | tf_op jit(solution)/shard_map/dot_general | solution.py:18
  (1 shorter events, 0.0 us)
Async XLA Ops:
  250.6 10.7 %slice-start = ((s8[6291456]{0:T(1024)(128)(4,1)}), s8[4194304]{0:T(1024)(128)(4,1)S(1)}, s32[]{:S(2)}) async-start(s8[6291456]{0:T(1024)(128)(4,1)} %bitcast.12), calls=%async_computation | async-start | bytes 8388608
  251.6 9.8 %slice-start.1 = ((s8[6291456]{0:T(1024)(128)(4,1)}), s8[2097152]{0:T(1024)(128)(4,1)S(1)}, s32[]{:S(2)}) async-start(s8[6291456]{0:T(1024)(128)(4,1)} %bitcast.12), calls=%async_computation.1 | async-start | bytes 4194304
  251.6 9.8 %copy-start = (bf16[1024,1536]{1,0:T(8,128)(2,1)S(1)}, bf16[1024,1536]{1,0:T(8,128)(2,1)}, u32[]{:S(2)}) copy-start(bf16[1024,1536]{1,0:T(8,128)(2,1)} %get-tuple-element.11) | copy-start | bytes 9437188

commit v3 on v2

--- a/solution.py
+++ b/solution.py
@@ -21,8 +21,8 @@
 
 
 MESH = pl.DeviceIdType.MESH
-TILE = 256
-SKEW = 2
+TILE = 128
+SKEW = 1
 
 
 def dot(a, b, ca, cb):

time: 268 us -> 227 us (0.85); the launches traced: 268 us -> 224 us
  Pallas kernels: 249 us -> 205 us
    pallas_call x1, Pallas kernels: 249 us -> 205 us  [fused(): pl.pallas_call(functools.partial(kernel, n), out_shape=(jax.ShapeDtypeStr...]
where the time goes in v3:
time: 227 us; the launch traced here: 224 us
  Pallas kernels  205 us (90%)
  matrix products  16.5 us (7%)
    pallas_call x1, Pallas kernels, fused(): pl.pallas_call(functools.partial(kernel, n), out_shape=(jax.ShapeDtypeStr...  205 us
    dot_general x2, matrix products, mm(): lax.dot_general(a, b, (((ca,), (cb,)), ((), ())), preferred_element_type=...  16.5 us

profile of v3, /device:TPU:0, one launch (start us, length us, event | category | flops | bytes accessed | tf_op | source)
XLA Modules:
  0.0 224.3 jit_solution(11786767376043016281)
XLA Ops:
  0.6 204.7 %shard_map.75 = (f32[2,256,768]{2,1,0:T(8,128)}, bf16[1024,1536]{1,0:T(8,128)(2,1)}, bf16[1024,1536]{1,0:T(8,128)(2,1)}, bf16[2,1024,1536]{2,1,0:T(8,128)(2,1)}) custom-call(bf16[256,768]{1,0:T(8,128)(2,1)} %tok_ref.1, bf16[256,768]{1,0:T(8,128)(2,1)} %cot_ref.1, bf16[1536,6144]{1,0:T(8,128)(2,1)} %win_hbm.1, bf16[6144,1536]{1,0:T(8,128)(2,1)} %wout_hbm.1), custom_call_target="tpu_custom_call" | custom-call | flops 19327352832 | bytes 9437184 | tf_op jit(solution)/shard_map/pallas_call | solution.py:246
  205.3 1.5 convert.4
  206.8 0.0 slice-start
  206.8 0.9 slice_bitcast_fusion
  207.7 0.0 slice-start.1
  207.7 0.0 copy-start
  207.7 9.7 %convolution_convert_fusion.1 = bf16[1536,1536]{1,0:T(8,128)(2,1)} fusion(bf16[1024,1536]{1,0:T(8,128)(2,1)} %get-tuple-element.9, bf16[2,1024,1536]{2,1,0:T(8,128)(2,1)} %get-tuple-element.10), kind=kOutput, calls=%fused_computation.1 | convolution fusion | flops 4834197504 | bytes 11010048 | tf_op jit(solution)/shard_map/dot_general | solution.py:18
  217.5 0.0 slice-done
  217.5 0.0 slice-done.1
  217.5 0.0 copy-done
  217.5 6.8 %convolution_convert_fusion = bf16[1536,1536]{1,0:T(8,128)(2,1)} fusion(bf16[1024,1536]{1,0:T(8,128)(2,1)S(1)} %copy-done, bf16[2,1024,1536]{2,1,0:T(8,128)(2,1)S(1)} %bitcast.13), kind=kOutput, calls=%fused_computation | convolution fusion | flops 4834197504 | bytes 11010048 | tf_op jit(solution)/shard_map/dot_general | solution.py:18
  (1 shorter events, 0.0 us)
Async XLA Ops:
  206.8 10.7 %slice-start = ((s8[6291456]{0:T(1024)(128)(4,1)}), s8[4194304]{0:T(1024)(128)(4,1)S(1)}, s32[]{:S(2)}) async-start(s8[6291456]{0:T(1024)(128)(4,1)} %bitcast.12), calls=%async_computation | async-start | bytes 8388608
  207.7 9.8 %slice-start.1 = ((s8[6291456]{0:T(1024)(128)(4,1)}), s8[2097152]{0:T(1024)(128)(4,1)S(1)}, s32[]{:S(2)}) async-start(s8[6291456]{0:T(1024)(128)(4,1)} %bitcast.12), calls=%async_computation.1 | async-start | bytes 4194304
  207.7 9.8 %copy-start = (bf16[1024,1536]{1,0:T(8,128)(2,1)S(1)}, bf16[1024,1536]{1,0:T(8,128)(2,1)}, u32[]{:S(2)}) copy-start(bf16[1024,1536]{1,0:T(8,128)(2,1)} %get-tuple-element.11) | copy-start | bytes 9437188
